TPU v7x, 32 devices: a whole 2x2x4 slice. The times are simulated.
32 devices in a mesh: gz: 8 (over y, x, core), gy: 4 (over z).
Axes of the slice: x: 2, y: 2, z: 4, core: 2. Of those that a mesh axis runs over, the one named last changes fastest.
Arguments:
- coarse_six: float32 [64, 1024, 512], P('gz', 'gy'), may hold values from 0.1 to 10
Outputs:
- detail_seven: float32 [64, 1024, 512], P('gz', 'gy')
- coarse_seven: float32 [64, 1024, 512], P('gz', 'gy')
All inputs are finite; a program needn't handle non-finite values.
Results may differ from a plain program's by a relative error of at most 0.00002.
Values sent between devices are 32-bit elements; how exact they have to be, the bound alone decides.
No kernel may reach another device: no remote copies, remote signals or barrier semaphores. Data moves between devices by JAX's collectives and lax.ppermute only.
A program may use at most 128 MiB of HBM per device.

v0:
```python
import functools
import math

import jax
import jax.numpy as jnp
from jax import lax
from jax.experimental import pallas as pl
from jax.experimental.pallas import tpu as pltpu
from jax.sharding import PartitionSpec as P

TAP_DILATION = 32
REACH = 2 * TAP_DILATION
LANES = 128
STRIP = 8
UNIT_ROWS = 128
FIRST_PLANES = 2
LEAD_UNITS = 2
LATER_GROUPS = (((2, 0),), ((2, 0),), ((1, 1), (1, 2)))
SHORT_FIRST = 2

kernel_weights = (0.0625, 0.25, 0.375, 0.25, 0.0625)


def passed_along(x, axis, by):
    peers = lax.axis_size(axis)
    return lax.ppermute(x, axis, [(i, (i + by) % peers) for i in range(peers)])


def z_taps(plane_stack, count):
    weights = {}
    for cell_position in range(5):
        filter_reach = (cell_position - 2) * TAP_DILATION // plane_stack
        moved = -filter_reach % count
        weights[moved] = weights.get(moved, 0.0) + kernel_weights[cell_position]
    own = weights.pop(0, 0.0)
    return own, weights


def lane_of(shape):
    return lax.broadcasted_iota(jnp.int32, shape, 1)


def x_taps():
    return {(cell_position - 2) * TAP_DILATION: kernel_weights[cell_position] for cell_position in range(5)}


def rest_taps():
    return {(cell_position - 2) * TAP_DILATION: weight for cell_position, weight in enumerate((0.125, 0.375, 0.375, 0.125))}


def pair_sums(rows):
    return (rows + pltpu.roll(rows, rows.shape[1] - TAP_DILATION, 1)) * 0.5


def fill_matrix(matrix_ref, taps):
    depth, width = matrix_ref.shape
    for start in range(0, depth, LANES):
        shape = (LANES, width)
        row = start + lax.broadcasted_iota(jnp.int32, shape, 0)
        offset = row - lax.broadcasted_iota(jnp.int32, shape, 1)
        offset = jnp.where(offset < 0, offset + width, offset)
        values = jnp.zeros(shape, jnp.float32)
        for tap, weight in taps.items():
            values = jnp.where(offset == tap % width, weight, values)
        matrix_ref[pl.ds(start, LANES), :] = values.astype(jnp.bfloat16)


def x_smoothed(rows, matrix):
    parts = []
    for _ in range(3):
        parts.append(rows.astype(jnp.bfloat16))
        rows = rows - parts[-1].astype(jnp.float32)
    terms = jnp.dot(jnp.concatenate(parts), matrix, preferred_element_type=jnp.float32)
    high, middle, low = jnp.split(terms, 3)
    return high + middle + low


def y_sums(groups):
    for _ in range(4):
        groups = [a + b for a, b in zip(groups[:-1], groups[1:])]
    return groups


def packed_rows(width):
    return UNIT_ROWS - UNIT_ROWS * TAP_DILATION // width


def store_packed(out_ref, place, smooth):
    rows, width = smooth.shape
    kept_rows = out_ref.shape[1]
    depth = rows - kept_rows
    out_ref[place, :, : width - LANES] = smooth[:kept_rows, : width - LANES]
    kept = lane_of((depth, LANES)) < LANES - TAP_DILATION
    for piece in range(kept_rows // depth):
        tile = piece * TAP_DILATION // LANES
        shift = (LANES - TAP_DILATION - piece * TAP_DILATION) % LANES
        moved = smooth[kept_rows:, tile * LANES : (tile + 1) * LANES]
        if shift:
            moved = pltpu.roll(moved, shift, 1)
        last = smooth[piece * depth : (piece + 1) * depth, width - LANES :]
        out_ref[place, pl.ds(piece * depth, depth), width - LANES :] = jnp.where(kept, last, moved)


def completed(strip):
    width = strip.shape[1]
    last = strip[:, width - LANES :]
    lane = lane_of(last.shape)
    kept = lane < LANES - TAP_DILATION
    total = jnp.where(kept, last, 0.0)
    for start in range(0, width - LANES, LANES):
        total = total + strip[:, start : start + LANES]
    odd = (lane // TAP_DILATION) % 2 == 1
    total = jnp.where(odd, -total, total)
    total = total + pltpu.roll(total, 2 * TAP_DILATION, 1)
    total = total + pltpu.roll(total, TAP_DILATION, 1)
    return jnp.concatenate([strip[:, : width - LANES], jnp.where(kept, last, total)], axis=1)


def unpacked(weights, refs, use):
    kept_rows, width = refs[0].shape[1:]
    depth = UNIT_ROWS - kept_rows
    tiles = [None] * (width // LANES)
    for piece in range(kept_rows // depth):
        rows = pl.ds(piece * depth, depth)
        strip = weighted(weights, [ref[0, rows, :] for ref in refs])
        tile = piece * TAP_DILATION // LANES
        shift = (piece * TAP_DILATION - (LANES - TAP_DILATION)) % LANES
        moved = strip[:, width - LANES :]
        if shift:
            moved = pltpu.roll(moved, shift, 1)
        if tiles[tile] is None:
            tiles[tile] = moved
        else:
            here = lane_of(moved.shape) // TAP_DILATION == piece % (LANES // TAP_DILATION)
            tiles[tile] = jnp.where(here, moved, tiles[tile])
        use(rows, completed(strip))
    use(pl.ds(kept_rows, depth), completed(jnp.concatenate(tiles, axis=1)))


def weighted(weights, values):
    total = None
    for weight, value in zip(weights, values):
        term = weight * value
        total = term if total is None else total + term
    return total


def pair_kernel(units_ref, out_ref, read_ref, read_sems):
    def read(unit):
        return pltpu.make_async_copy(units_ref.at[unit], read_ref.at[unit], read_sems.at[unit])

    for unit in range(out_ref.shape[0]):
        read(unit).start()
    for unit in range(out_ref.shape[0]):
        read(unit).wait()
        store_packed(out_ref, unit, pair_sums(read_ref[unit]))


def x_kernel(first, units_ref, out_ref, read_ref, matrix_ref, read_sems):
    count = out_ref.shape[0]

    def read(unit):
        return pltpu.make_async_copy(units_ref.at[first + unit], read_ref.at[unit], read_sems.at[unit])

    for unit in range(count):
        read(unit).start()
    fill_matrix(matrix_ref, x_taps())

    @pl.loop(0, count)
    def _(unit):
        read(unit).wait()
        store_packed(out_ref, unit, x_smoothed(read_ref[unit], matrix_ref[...]))


def extended_groups(before_ref, c_ref, after_ref, offset):
    groups = []
    for ref in (before_ref, c_ref, after_ref):
        for start in range(0, ref.shape[1], TAP_DILATION):
            groups.append(ref[0, pl.ds(start + offset, STRIP), :])
    return groups


def y_smoothed(before_ref, c_ref, after_ref, smooth_ref):
    for within in range(TAP_DILATION // STRIP):
        groups = y_sums(extended_groups(before_ref, c_ref, after_ref, within * STRIP))
        for group, strip in enumerate(groups):
            smooth_ref[pl.ds(group * TAP_DILATION + within * STRIP, STRIP), :] = strip * (1.0 / 16.0)


def yx_kernel(before_ref, c_ref, after_ref, *refs):
    *out_refs, matrix_ref, smooth_ref = refs
    pl.when(pl.program_id(0) == 0)(lambda: fill_matrix(matrix_ref, x_taps()))
    y_smoothed(before_ref, c_ref, after_ref, smooth_ref)
    places = [(ref, place) for ref in out_refs for place in range(ref.shape[0])]
    for unit, (ref, place) in enumerate(places):
        smooth = x_smoothed(smooth_ref[pl.ds(unit * UNIT_ROWS, UNIT_ROWS), :], matrix_ref[...])
        store_packed(ref, place, smooth)


def z_kernel(weights, *refs):
    whole_ref = refs[-1]

    def use(rows, strip):
        whole_ref[0, rows, :] = strip

    unpacked(weights, refs[: len(weights)], use)


def group_of(shape):
    return lane_of(shape) // TAP_DILATION


def spread(tile, group):
    tile = jnp.where(group_of(tile.shape) == group, tile, 0.0)
    tile = tile + pltpu.roll(tile, 2 * TAP_DILATION, 1)
    return tile + pltpu.roll(tile, TAP_DILATION, 1)


def strip_rows(rows, ahead):
    per_group = TAP_DILATION // STRIP
    strip = lax.rem(lax.axis_index("gy") + ahead, per_group)
    return pl.ds(pl.multiple_of(rows - TAP_DILATION + strip * STRIP, STRIP), STRIP)


def short_strips(rows):
    half = rows - UNIT_ROWS
    fixed = [pl.ds(row, STRIP) for row in range(0, rows - TAP_DILATION, STRIP)]
    moving = [strip_rows(rows, ahead) for ahead in range(1, TAP_DILATION // STRIP)]
    return fixed[: half // STRIP], fixed[half // STRIP :] + moving


def short_tiles(rows, width):
    return (rows // STRIP - 3) * (width // LANES)


def short_kernel(before_ref, c_ref, after_ref, out_ref, matrix_ref, smooth_ref):
    plane = pl.program_id(0)

    @pl.when(plane == 0)
    def _():
        fill_matrix(matrix_ref, x_taps())
        out_ref[out_ref.shape[0] - 1] = jnp.zeros((STRIP, LANES), jnp.float32)

    y_smoothed(before_ref, c_ref, after_ref, smooth_ref)
    rows, width = smooth_ref.shape
    for start in range(0, rows, UNIT_ROWS):
        unit = pl.ds(start, UNIT_ROWS)
        smooth_ref[unit, :] = x_smoothed(smooth_ref[unit, :], matrix_ref[...])
    index = plane * short_tiles(rows, width)
    groups = LANES // TAP_DILATION
    for places in short_strips(rows):
        *places, last_place = places
        last = smooth_ref[last_place, :]
        for piece, place in enumerate(places):
            strip = smooth_ref[place, :]
            tile = piece // groups * LANES
            moved = last[:, tile : tile + LANES]
            shift = (groups - 1 - piece) % groups * TAP_DILATION
            if shift:
                moved = pltpu.roll(moved, shift, 1)
            for start in range(0, width - LANES, LANES):
                out_ref[index] = strip[:, start : start + LANES]
                index += 1
            here = group_of(moved.shape) == groups - 1
            out_ref[index] = jnp.where(here, moved, strip[:, width - LANES :])
            index += 1
    left = spread(last[:, width - LANES :], groups - 2)
    end = out_ref.shape[0] - 1
    out_ref[end] = jnp.where(group_of(left.shape) == plane, left, out_ref[end])


def short_z_kernel(weights, *refs):
    packed, (whole_ref, *sum_refs) = refs[: len(weights)], refs[-4:]
    rows, width = whole_ref.shape[1:]
    plane = pl.program_id(0)
    index = plane * short_tiles(rows, width)
    groups, tiles = LANES // TAP_DILATION, width // LANES
    for places in short_strips(rows):
        *places, last_place = places
        last = [None] * tiles
        for piece, place in enumerate(places):
            strip = [weighted(weights, [ref[index + tile] for ref in packed]) for tile in range(tiles)]
            index += tiles
            tile, group = divmod(piece, groups)
            shift = (group + 1 - groups) % groups * TAP_DILATION
            moved = pltpu.roll(strip[-1], shift, 1) if shift else strip[-1]
            here = group_of(moved.shape) == group
            last[tile] = moved if last[tile] is None else jnp.where(here, moved, last[tile])
            whole_ref[0, place, :] = completed(jnp.concatenate(strip, axis=1))
        if len(places) < tiles * groups - 1:
            end = packed[0].shape[0] - 1
            left = spread(weighted(weights, [ref[end] for ref in packed]), plane)
            last[-1] = jnp.where(group_of(left.shape) == groups - 2, left, last[-1])
        whole_ref[0, last_place, :] = completed(jnp.concatenate(last, axis=1))

    groups = rows // TAP_DILATION
    for ahead in range(TAP_DILATION // STRIP):
        total = None
        for group in range(groups if ahead else groups - 1):
            strip = whole_ref[0, strip_rows((group + 1) * TAP_DILATION, ahead), :]
            if total is None:
                total = strip
            else:
                total = total + strip if group % 2 == 0 else total - strip
        if ahead:
            sum_refs[ahead - 1][0] = total
        else:
            whole_ref[0, strip_rows(rows, 0), :] = total


def short_finish_kernel(whole_ref, *refs):
    *sum_refs, c_ref, _, _, detail_ref, coarse_ref = refs
    missing = strip_rows(whole_ref.shape[1], 0)
    coarse_ref[...] = whole_ref[...]
    coarse_ref[0, missing, :] = whole_ref[0, missing, :] + sum(ref[0] for ref in sum_refs)
    detail_ref[...] = c_ref[...] - coarse_ref[...]


def pair_z_kernel(weights, *refs):
    whole_ref, matrix_ref, pair_ref = refs[-3:]
    pl.when(pl.program_id(0) == 0)(lambda: fill_matrix(matrix_ref, rest_taps()))

    def use(rows, strip):
        pair_ref[rows, :] = strip

    unpacked(weights, refs[: len(weights)], use)
    whole_ref[0] = x_smoothed(pair_ref[...], matrix_ref[...])


def y_kernel(before_ref, whole_ref, after_ref, c_ref, detail_ref, coarse_ref):
    scale = 1.0 / 16.0
    for within in range(TAP_DILATION // STRIP):
        groups = y_sums(extended_groups(before_ref, whole_ref, after_ref, within * STRIP))
        for group, strip in enumerate(groups):
            rows = pl.ds(group * TAP_DILATION + within * STRIP, STRIP)
            coarse = strip * scale
            coarse_ref[0, rows, :] = coarse
            detail_ref[0, rows, :] = c_ref[0, rows, :] - coarse


def finish_kernel(weights, *refs):
    c_ref, _, _, detail_ref, coarse_ref = refs[len(weights) :]

    def use(rows, strip):
        coarse_ref[0, rows, :] = strip
        detail_ref[0, rows, :] = c_ref[0, rows, :] - strip

    unpacked(weights, refs[: len(weights)], use)


def last_kernel(weights, place, *refs):
    units_ref, _, _, detail_ref, coarse_ref, results_ref, write_sems = refs[len(weights) :]
    half = UNIT_ROWS // 2

    def write(piece, output, ref):
        rows = pl.ds(piece * half, half)
        source = results_ref.at[output, rows]
        return pltpu.make_async_copy(source, ref.at[place, rows], write_sems.at[piece, output])

    writes = [[write(piece, 0, detail_ref), write(piece, 1, coarse_ref)] for piece in range(2)]

    def use(rows, strip):
        results_ref[1, rows, :] = strip
        results_ref[0, rows, :] = units_ref[place, rows, :] - strip
        piece, left = divmod(rows.start + rows.size, half)
        if left == 0:
            for copy in writes[piece - 1]:
                copy.start()

    unpacked(weights, refs[: len(weights)], use)
    for copies in writes:
        for copy in copies:
            copy.wait()


def block_of(rows, width, first=0, depth=1):
    return pl.BlockSpec((depth, rows, width), lambda step: (first + step, 0, 0))


def anywhere():
    return pl.BlockSpec(memory_space=pl.ANY)


def tiles_of(pieces):
    return pl.BlockSpec((pieces, STRIP, LANES), lambda step: (0, 0, 0))


def in_vmem():
    return pl.BlockSpec(memory_space=pltpu.VMEM)


def call(kernel, name, steps, in_specs, out_specs, out_shape, args, aliases=None, scratch=(), grant=24):
    blocks = [spec.block_shape for spec in (*in_specs, *out_specs) if spec.block_shape]
    moved = 4 * max(steps, 1) * sum(math.prod(block) for block in blocks)
    return pl.pallas_call(
        kernel,
        grid=(steps,) if steps else (),
        in_specs=in_specs,
        out_specs=out_specs,
        out_shape=out_shape,
        scratch_shapes=scratch,
        input_output_aliases=aliases or {},
        compiler_params=pltpu.CompilerParams(vmem_limit_bytes=grant * 1024 * 1024),
        cost_estimate=pl.CostEstimate(flops=moved * 2, bytes_accessed=moved, transcendentals=0),
        name=name,
    )(*args)


def in_hbm(x):
    return pltpu.with_memory_space_constraint(x, pltpu.HBM)


def f32(*shape):
    return jax.ShapeDtypeStruct(shape, jnp.float32)


def can_shorten(rows, width):
    strips = TAP_DILATION // STRIP
    return lax.axis_size("gy") == strips and rows // TAP_DILATION % 2 == 0 and UNIT_ROWS // STRIP == width // TAP_DILATION


def shards(coarse_six):
    planes, rows, width = coarse_six.shape
    short = packed_rows(width)
    own, shifts = z_taps(planes, lax.axis_size("gz"))
    weights = (own, *shifts.values())
    count = len(weights)
    whole, unit, packed, edge = (functools.partial(block_of, n, width) for n in (rows, UNIT_ROWS, short, REACH))
    parts = rows // UNIT_ROWS
    units = coarse_six.reshape(planes * parts, UNIT_ROWS, width)
    matrix = pltpu.VMEM((width, width), jnp.bfloat16)

    def along_gz(x):
        return [passed_along(x, "gz", moved) for moved in shifts]

    def halo(source, start, stop):
        top, bottom = source[start:stop, :REACH], source[start:stop, rows - REACH :]
        return passed_along(bottom, "gy", 1), passed_along(top, "gy", -1)

    sums_shape = f32(FIRST_PLANES * parts, UNIT_ROWS, width)
    lead = call(
        pair_kernel,
        "pair_x",
        0,
        [anywhere()],
        [in_vmem()],
        [pltpu.VMEM((LEAD_UNITS, short, width), jnp.float32)],
        [in_hbm(units)],
        scratch=[pltpu.VMEM((LEAD_UNITS, UNIT_ROWS, width), jnp.float32), pltpu.SemaphoreType.DMA((LEAD_UNITS,))],
    )[0]
    lead, ready = lax.optimization_barrier((lead, units))
    lead_moved = along_gz(lead)
    first = FIRST_PLANES * parts - LEAD_UNITS
    first_block = call(
        functools.partial(x_kernel, LEAD_UNITS),
        "smooth_x",
        0,
        [anywhere()],
        [in_vmem()],
        [pltpu.VMEM((first, short, width), jnp.float32)],
        [in_hbm(ready)],
        scratch=[
            pltpu.VMEM((first, UNIT_ROWS, width), jnp.float32),
            matrix,
            pltpu.SemaphoreType.DMA((first,)),
        ],
    )[0]
    first_block, ready = lax.optimization_barrier((first_block, coarse_six))
    first_moved = along_gz(first_block)
    sums = call(
        functools.partial(pair_z_kernel, weights),
        "smooth_zx",
        LEAD_UNITS,
        [packed()] * count,
        [unit()],
        [sums_shape],
        [lead, *lead_moved],
        scratch=[matrix, pltpu.VMEM((UNIT_ROWS, width), jnp.float32)],
    )

    later, short_sent = [], []
    start = FIRST_PLANES
    near = halo(ready, start, start + sum(size for size, _ in LATER_GROUPS[0]))
    near, sums = lax.optimization_barrier((near, sums))
    for number, sizes in enumerate(LATER_GROUPS):
        offset = 0
        for size, messages in sizes:
            place = start + offset
            sources = [near[0], in_hbm(coarse_six), near[1]]
            specs = [edge(offset), whole(place), edge(offset)]
            scratch = [matrix, pltpu.VMEM((rows, width), jnp.float32)]
            if messages or not can_shorten(rows, width):
                messages = max(messages, 1)
                depth = parts // messages
                blocks = call(
                    yx_kernel,
                    "smooth_yx",
                    size,
                    specs,
                    [packed(depth=depth)] * messages,
                    [f32(size * depth, short, width)] * messages,
                    sources,
                    scratch=scratch,
                )
                for message, block in enumerate(blocks):
                    last_block = block
                    later.append((place * parts + message * depth, size * depth, (block, *along_gz(block))))
            else:
                pieces = size * short_tiles(rows, width) + 1
                block = call(
                    short_kernel,
                    "smooth_yx_short",
                    size,
                    specs,
                    [tiles_of(pieces)],
                    [f32(pieces, STRIP, LANES)],
                    sources,
                    scratch=scratch,
                )[0]
                short_sent.append((place, size, (block, *along_gz(block))))
            offset += size
        start += offset
        if number == 0:
            block, ready = lax.optimization_barrier((block, ready))
            block, *first_moved = lax.optimization_barrier((block, *first_moved))
            sums = call(
                functools.partial(z_kernel, weights),
                "smooth_z",
                first,
                [packed()] * count + [anywhere()],
                [unit(LEAD_UNITS)],
                [sums_shape],
                [first_block, *first_moved, *sums],
                {count: 0},
            )[0]
            along_z = sums.reshape(FIRST_PLANES, rows, width)
            along_z, ready = lax.optimization_barrier((along_z, ready))
        if number + 1 < len(LATER_GROUPS):
            if not number:
                block, ready = lax.optimization_barrier((block, ready))
            near = halo(ready, start, start + sum(size for size, _ in LATER_GROUPS[number + 1]))
        if number == 1:
            first_near, along_z, _ = lax.optimization_barrier((near[0], along_z, short_sent[0][2]))
            near = (first_near, near[1])
            sides = halo(along_z, 0, FIRST_PLANES)
        if number == 0:
            near, along_z = lax.optimization_barrier((near, along_z))

    def sum_short(batch):
        planes_in = sum(size for _, size, _ in batch)
        step, sums = 0, []
        for _, size, blocks in batch:
            sums = call(
                functools.partial(short_z_kernel, weights),
                "smooth_z_short",
                size,
                [tiles_of(blocks[0].shape[0])] * count + [anywhere()] * len(sums),
                [whole(step)] + [block_of(STRIP, width, step)] * 3,
                [f32(planes_in, rows, width)] + [f32(planes_in, STRIP, width)] * 3,
                [*blocks, *sums],
                {count + at: at for at in range(len(sums))},
            )
            step += size
        return sums[0], [passed_along(total, "gy", ahead) for ahead, total in enumerate(sums[1:], 1)]

    def finish_short(batch, sums, outs):
        start, size = batch[0][0], sum(size for _, size, _ in batch)
        along_z, moved = sums
        outs, moved = lax.optimization_barrier((outs, moved))
        return call(
            short_finish_kernel,
            "finish_short",
            size,
            [whole()] + [block_of(STRIP, width)] * 3 + [whole(start)] + [anywhere()] * 2,
            [whole(start)] * 2,
            [f32(planes, rows, width)] * 2,
            [along_z, *moved, coarse_six, *outs],
            {5: 0, 6: 1},
        )

    batches = [batch for batch in (short_sent[:SHORT_FIRST], short_sent[SHORT_FIRST:]) if batch]
    batch = batches[0]
    short_sums = sum_short(batch)
    short_whole, sides = lax.optimization_barrier((short_sums[0], sides))
    outs = call(
        y_kernel,
        "smooth_y",
        FIRST_PLANES,
        [edge(), whole(), edge(), whole()],
        [whole(), whole()],
        [f32(planes, rows, width)] * 2,
        [sides[0], along_z, sides[1], coarse_six],
    )
    short_sums, last_block = lax.optimization_barrier(((short_whole, short_sums[1]), last_block))
    last_moved = along_gz(last_block)
    outs = finish_short(batch, short_sums, outs)
    outs = [out.reshape(units.shape) for out in outs]
    for place, size, blocks in later[:-1]:
        outs, blocks = lax.optimization_barrier((outs, blocks))
        outs = call(
            functools.partial(finish_kernel, weights),
            "finish",
            size,
            [packed()] * count + [unit(place)] + [anywhere()] * 2,
            [unit(place)] * 2,
            [f32(*units.shape)] * 2,
            [*blocks, units, *outs],
            {count + 1: 0, count + 2: 1},
        )
    place = later[-1][0]
    blocks = (last_block, *last_moved)
    outs, blocks = lax.optimization_barrier((outs, blocks))
    outs = call(
        functools.partial(last_kernel, weights, place),
        "finish_last",
        0,
        [in_vmem()] * (count + 1) + [anywhere()] * 2,
        [anywhere()] * 2,
        [f32(*units.shape)] * 2,
        [*blocks, units, *outs],
        {count + 1: 0, count + 2: 1},
        scratch=[
            pltpu.VMEM((2, UNIT_ROWS, width), jnp.float32),
            pltpu.SemaphoreType.DMA((2, 2)),
        ],
    )
    return tuple(out.reshape(coarse_six.shape) for out in outs)


def solution(mesh):
    return jax.shard_map(
        shards,
        mesh=mesh,
        in_specs=(P("gz", "gy", None),),
        out_specs=(P("gz", "gy", None), P("gz", "gy", None)),
        check_vma=False,
    )
```

profile of v0, /device:TPU:0, one launch (start us, length us, event | category | flops | bytes accessed | tf_op | source)
XLA Modules:
  0.0 91.0 jit_solution(4105577332467227477)
XLA Ops:
  0.6 1.3 %pair_x.1.refs_0_ = f32[2,120,512]{2,1,0:T(8,128)S(1)} custom-call(f32[16,128,512]{2,1,0:T(8,128)} %bitcast.6), custom_call_target="tpu_custom_call" | custom-call | tf_op jit(solution)/shard_map/pair_x/pallas_call | solution.py:395
  1.9 3.0 %collective-permute-start.3 = (f32[2,120,512]{2,1,0:T(8,128)S(1)}, f32[2,120,512]{2,1,0:T(8,128)S(1)}, u32[]{:S(2)}, u32[]{:S(2)}) collective-permute-start(f32[2,120,512]{2,1,0:T(8,128)S(1)} %pair_x.1.refs_0_), channel_id=1, source_target_pairs={{0,16},{4,20},{8,24},{12,28},{16,0},{20,4},{24,8},{28,12},{1,17},{... | collective-permute-start | bytes 1474568 | tf_op jit(solution)/shard_map/ppermute | solution.py:26
  5.0 1.9 %smooth_x.1.refs_0_ = f32[2,120,512]{2,1,0:T(8,128)S(1)} custom-call(f32[16,128,512]{2,1,0:T(8,128)} %bitcast.7), custom_call_target="tpu_custom_call" | custom-call | tf_op jit(solution)/shard_map/smooth_x/pallas_call | solution.py:395
  6.9 0.1 collective-permute-start
  6.9 1.1 %fusion.1 = (f32[2,64,512]{2,1,0:T(8,128)S(1)}, f32[2,64,512]{2,1,0:T(8,128)S(1)}) fusion(f32[8,256,512]{2,1,0:T(8,128)} %c_ref.9), kind=kLoop, calls=%fused_computation.1 | loop fusion | bytes 1048576 | tf_op jit(solution)/shard_map/slice | solution.py:437
  8.0 2.1 %collective-permute-start.1 = (f32[2,64,512]{2,1,0:T(8,128)S(1)}, f32[2,64,512]{2,1,0:T(8,128)S(1)}, u32[]{:S(2)}, u32[]{:S(2)}) collective-permute-start(f32[2,64,512]{2,1,0:T(8,128)S(1)} %get-tuple-element.127), channel_id=1, source_target_pairs={{0,1},{1,2},{2,3},{3,0},{4,5},{5,6},{6,7},{7,4},{8,9},{9,10},{10,1... | collective-permute-start | bytes 786440 | tf_op jit(solution)/shard_map/ppermute | solution.py:26
  10.1 2.1 %collective-permute-start.2 = (f32[2,64,512]{2,1,0:T(8,128)S(1)}, f32[2,64,512]{2,1,0:T(8,128)S(1)}, u32[]{:S(2)}, u32[]{:S(2)}) collective-permute-start(f32[2,64,512]{2,1,0:T(8,128)S(1)} %get-tuple-element.126), channel_id=1, source_target_pairs={{0,3},{1,0},{2,1},{3,2},{4,7},{5,4},{6,5},{7,6},{8,11},{9,8},{10,9... | collective-permute-start | bytes 786440 | tf_op jit(solution)/shard_map/ppermute | solution.py:26
  12.2 4.8 %collective-permute-done.3.refs_1_ = f32[2,120,512]{2,1,0:T(8,128)S(1)} collective-permute-done((f32[2,120,512]{2,1,0:T(8,128)S(1)}, f32[2,120,512]{2,1,0:T(8,128)S(1)}, u32[]{:S(2)}, u32[]{:S(2)}) %collective-permute-start.3) | collective-permute-done | bytes 491552 | tf_op jit(solution)/shard_map/ppermute | solution.py:26
  17.0 1.1 %smooth_zx.1.refs_2_ = f32[4,128,512]{2,1,0:T(8,128)S(1)} custom-call(f32[2,120,512]{2,1,0:T(8,128)S(1)} %pair_x.1.refs_0_, f32[2,120,512]{2,1,0:T(8,128)S(1)} %collective-permute-done.3.refs_1_), custom_call_target="tpu_custom_call" | custom-call | flops 3014656 | bytes 1507328 | tf_op jit(solution)/shard_map/smooth_zx/pallas_call | solution.py:395
  18.1 1.3 %collective-permute-done.1.before_ref = f32[2,64,512]{2,1,0:T(8,128)S(1)} collective-permute-done((f32[2,64,512]{2,1,0:T(8,128)S(1)}, f32[2,64,512]{2,1,0:T(8,128)S(1)}, u32[]{:S(2)}, u32[]{:S(2)}) %collective-permute-start.1) | collective-permute-done | bytes 262176 | tf_op jit(solution)/shard_map/ppermute | solution.py:26
  19.4 3.5 %collective-permute-done.2.after_ref = f32[2,64,512]{2,1,0:T(8,128)S(1)} collective-permute-done((f32[2,64,512]{2,1,0:T(8,128)S(1)}, f32[2,64,512]{2,1,0:T(8,128)S(1)}, u32[]{:S(2)}, u32[]{:S(2)}) %collective-permute-start.2) | collective-permute-done | bytes 262176 | tf_op jit(solution)/shard_map/ppermute | solution.py:26
  22.9 2.7 %smooth_yx_short.2.refs_0_ = f32[233,8,128]{2,1,0:T(8,128)S(1)} custom-call(f32[2,64,512]{2,1,0:T(8,128)S(1)} %collective-permute-done.1.before_ref, f32[8,256,512]{2,1,0:T(8,128)} %c_ref.9, f32[2,64,512]{2,1,0:T(8,128)S(1)} %collective-permute-done.2.after_ref), custom_call_target="tpu_custom_call" | custom-call | flops 6963200 | bytes 3481600 | tf_op jit(solution)/shard_map/smooth_yx_short/pallas_call | solution.py:395
  25.7 1.6 %collective-permute-start.7 = (f32[233,8,128]{2,1,0:T(8,128)S(1)}, f32[233,8,128]{2,1,0:T(8,128)S(1)}, u32[]{:S(2)}, u32[]{:S(2)}) collective-permute-start(f32[233,8,128]{2,1,0:T(8,128)S(1)} %smooth_yx_short.2.refs_0_), channel_id=1, source_target_pairs={{0,16},{4,20},{8,24},{12,28},{16,0},{20,4},{24,8},{28,12},{1,17},{... | collective-permute-start | bytes 2863112 | tf_op jit(solution)/shard_map/ppermute | solution.py:26
  27.2 0.0 collective-permute-done.refs_1_
  27.2 0.5 smooth_z.1
  27.7 1.3 %fusion = (f32[2,64,512]{2,1,0:T(8,128)S(1)}, f32[2,64,512]{2,1,0:T(8,128)S(1)}, f32[2,64,512]{2,1,0:T(8,128)S(1)}, f32[2,64,512]{2,1,0:T(8,128)S(1)}) fusion(f32[8,256,512]{2,1,0:T(8,128)} %c_ref.9), kind=kLoop, calls=%fused_computation | loop fusion | bytes 2097152 | tf_op jit(solution)/shard_map/slice | solution.py:437
  29.0 1.3 %collective-permute-start.4 = (f32[2,64,512]{2,1,0:T(8,128)S(1)}, f32[2,64,512]{2,1,0:T(8,128)S(1)}, u32[]{:S(2)}, u32[]{:S(2)}) collective-permute-start(f32[2,64,512]{2,1,0:T(8,128)S(1)} %get-tuple-element.125), channel_id=1, source_target_pairs={{0,1},{1,2},{2,3},{3,0},{4,5},{5,6},{6,7},{7,4},{8,9},{9,10},{10,1... | collective-permute-start | bytes 786440 | tf_op jit(solution)/shard_map/ppermute | solution.py:26
  30.3 3.2 %collective-permute-start.5 = (f32[2,64,512]{2,1,0:T(8,128)S(1)}, f32[2,64,512]{2,1,0:T(8,128)S(1)}, u32[]{:S(2)}, u32[]{:S(2)}) collective-permute-start(f32[2,64,512]{2,1,0:T(8,128)S(1)} %get-tuple-element.124), channel_id=1, source_target_pairs={{0,3},{1,0},{2,1},{3,2},{4,7},{5,4},{6,5},{7,6},{8,11},{9,8},{10,9... | collective-permute-start | bytes 786440 | tf_op jit(solution)/shard_map/ppermute | solution.py:26
  33.5 7.2 %collective-permute-done.4.before_ref = f32[2,64,512]{2,1,0:T(8,128)S(1)} collective-permute-done((f32[2,64,512]{2,1,0:T(8,128)S(1)}, f32[2,64,512]{2,1,0:T(8,128)S(1)}, u32[]{:S(2)}, u32[]{:S(2)}) %collective-permute-start.4) | collective-permute-done | bytes 262176 | tf_op jit(solution)/shard_map/ppermute | solution.py:26
  40.7 2.7 %collective-permute-done.5.after_ref = f32[2,64,512]{2,1,0:T(8,128)S(1)} collective-permute-done((f32[2,64,512]{2,1,0:T(8,128)S(1)}, f32[2,64,512]{2,1,0:T(8,128)S(1)}, u32[]{:S(2)}, u32[]{:S(2)}) %collective-permute-start.5) | collective-permute-done | bytes 262176 | tf_op jit(solution)/shard_map/ppermute | solution.py:26
  43.5 2.7 %smooth_yx_short.3.refs_0_ = f32[233,8,128]{2,1,0:T(8,128)S(1)} custom-call(f32[2,64,512]{2,1,0:T(8,128)S(1)} %collective-permute-done.4.before_ref, f32[8,256,512]{2,1,0:T(8,128)} %c_ref.9, f32[2,64,512]{2,1,0:T(8,128)S(1)} %collective-permute-done.5.after_ref), custom_call_target="tpu_custom_call" | custom-call | flops 6963200 | bytes 3481600 | tf_op jit(solution)/shard_map/smooth_yx_short/pallas_call | solution.py:395
  46.2 0.9 %collective-permute-start.6 = (f32[233,8,128]{2,1,0:T(8,128)S(1)}, f32[233,8,128]{2,1,0:T(8,128)S(1)}, u32[]{:S(2)}, u32[]{:S(2)}) collective-permute-start(f32[233,8,128]{2,1,0:T(8,128)S(1)} %smooth_yx_short.3.refs_0_), channel_id=1, source_target_pairs={{0,16},{4,20},{8,24},{12,28},{16,0},{20,4},{24,8},{28,12},{1,17},{... | collective-permute-start | bytes 2863112 | tf_op jit(solution)/shard_map/ppermute | solution.py:26
  47.1 1.1 %collective-permute-start.8 = (f32[2,64,512]{2,1,0:T(8,128)S(1)}, f32[2,64,512]{2,1,0:T(8,128)S(1)}, u32[]{:S(2)}, u32[]{:S(2)}) collective-permute-start(f32[2,64,512]{2,1,0:T(8,128)S(1)} %get-tuple-element.123), channel_id=1, source_target_pairs={{0,1},{1,2},{2,3},{3,0},{4,5},{5,6},{6,7},{7,4},{8,9},{9,10},{10,1... | collective-permute-start | bytes 786440 | tf_op jit(solution)/shard_map/ppermute | solution.py:26
  48.2 2.7 %collective-permute-start.14 = (f32[2,64,512]{2,1,0:T(8,128)S(1)}, f32[2,64,512]{2,1,0:T(8,128)S(1)}, u32[]{:S(2)}, u32[]{:S(2)}) collective-permute-start(f32[2,64,512]{2,1,0:T(8,128)S(1)} %get-tuple-element.122), channel_id=1, source_target_pairs={{0,3},{1,0},{2,1},{3,2},{4,7},{5,4},{6,5},{7,6},{8,11},{9,8},{10,9... | collective-permute-start | bytes 786440 | tf_op jit(solution)/shard_map/ppermute | solution.py:26
  50.9 7.2 %collective-permute-done.8.before_ref = f32[2,64,512]{2,1,0:T(8,128)S(1)} collective-permute-done((f32[2,64,512]{2,1,0:T(8,128)S(1)}, f32[2,64,512]{2,1,0:T(8,128)S(1)}, u32[]{:S(2)}, u32[]{:S(2)}) %collective-permute-start.8) | collective-permute-done | bytes 262176 | tf_op jit(solution)/shard_map/ppermute | solution.py:26
  58.2 0.0 collective-permute-done.7.refs_1_
  58.2 0.1 collective-permute-start.10
  58.3 2.0 %collective-permute-start.9 = (f32[2,64,512]{2,1,0:T(8,128)S(1)}, f32[2,64,512]{2,1,0:T(8,128)S(1)}, u32[]{:S(2)}, u32[]{:S(2)}) collective-permute-start(f32[2,64,512]{2,1,0:T(8,128)S(1)} %get-tuple-element.129), channel_id=1, source_target_pairs={{0,1},{1,2},{2,3},{3,0},{4,5},{5,6},{6,7},{7,4},{8,9},{9,10},{10,1... | collective-permute-start | bytes 786440 | tf_op jit(solution)/shard_map/ppermute | solution.py:26
  60.3 1.7 %collective-permute-done.14.after_ref = f32[2,64,512]{2,1,0:T(8,128)S(1)} collective-permute-done((f32[2,64,512]{2,1,0:T(8,128)S(1)}, f32[2,64,512]{2,1,0:T(8,128)S(1)}, u32[]{:S(2)}, u32[]{:S(2)}) %collective-permute-start.14) | collective-permute-done | bytes 262176 | tf_op jit(solution)/shard_map/ppermute | solution.py:26
  62.0 1.9 %smooth_yx.3.refs_0_ = f32[2,120,512]{2,1,0:T(8,128)S(1)} custom-call(f32[2,64,512]{2,1,0:T(8,128)S(1)} %collective-permute-done.8.before_ref, f32[8,256,512]{2,1,0:T(8,128)} %c_ref.9, f32[2,64,512]{2,1,0:T(8,128)S(1)} %collective-permute-done.14.after_ref), custom_call_target="tpu_custom_call" | custom-call | flops 2555904 | bytes 1277952 | tf_op jit(solution)/shard_map/smooth_yx/pallas_call | solution.py:395
  63.9 1.5 %collective-permute-start.15 = (f32[2,120,512]{2,1,0:T(8,128)S(1)}, f32[2,120,512]{2,1,0:T(8,128)S(1)}, u32[]{:S(2)}, u32[]{:S(2)}) collective-permute-start(f32[2,120,512]{2,1,0:T(8,128)S(1)} %smooth_yx.3.refs_0_), channel_id=1, source_target_pairs={{0,16},{4,20},{8,24},{12,28},{16,0},{20,4},{24,8},{28,12},{1,17},{... | collective-permute-start | bytes 1474568 | tf_op jit(solution)/shard_map/ppermute | solution.py:26
  65.4 0.7 smooth_z_short.2
  66.1 4.2 %collective-permute-done.6.refs_1_ = f32[233,8,128]{2,1,0:T(8,128)S(1)} collective-permute-done((f32[233,8,128]{2,1,0:T(8,128)S(1)}, f32[233,8,128]{2,1,0:T(8,128)S(1)}, u32[]{:S(2)}, u32[]{:S(2)}) %collective-permute-start.6) | collective-permute-done | bytes 954400 | tf_op jit(solution)/shard_map/ppermute | solution.py:26
  70.3 0.0 copy-start
  70.3 0.7 smooth_z_short.3
  71.0 0.8 collective-permute-start.11
  71.8 2.1 %collective-permute-start.12 = (f32[4,8,512]{2,1,0:T(8,128)S(1)}, f32[4,8,512]{2,1,0:T(8,128)S(1)}, u32[]{:S(2)}, u32[]{:S(2)}) collective-permute-start(f32[4,8,512]{2,1,0:T(8,128)S(1)} %get-tuple-element.83), channel_id=1, source_target_pairs={{0,2},{1,3},{2,0},{3,1},{4,6},{5,7},{6,4},{7,5},{8,10},{9,11},{10,... | collective-permute-start | bytes 196616 | tf_op jit(solution)/shard_map/ppermute | solution.py:26
  73.9 0.0 collective-permute-done.10.after_ref
  73.9 1.3 %collective-permute-start.13 = (f32[4,8,512]{2,1,0:T(8,128)S(1)}, f32[4,8,512]{2,1,0:T(8,128)S(1)}, u32[]{:S(2)}, u32[]{:S(2)}) collective-permute-start(f32[4,8,512]{2,1,0:T(8,128)S(1)} %get-tuple-element.84), channel_id=1, source_target_pairs={{0,3},{1,0},{2,1},{3,2},{4,7},{5,4},{6,5},{7,6},{8,11},{9,8},{10,9... | collective-permute-start | bytes 196616 | tf_op jit(solution)/shard_map/ppermute | solution.py:26
  75.2 1.9 %smooth_yx.2 = (f32[1,120,512]{2,1,0:T(8,128)S(1)}, f32[1,120,512]{2,1,0:T(8,128)S(1)}) custom-call(f32[2,64,512]{2,1,0:T(8,128)S(1)} %collective-permute-done.8.before_ref, f32[8,256,512]{2,1,0:T(8,128)} %c_ref.9, f32[2,64,512]{2,1,0:T(8,128)S(1)} %collective-permute-done.14.after_ref), custom_call_target="tpu_custom_call" | custom-call | flops 2555904 | bytes 1277952 | tf_op jit(solution)/shard_map/smooth_yx/pallas_call | solution.py:395
  77.1 0.0 collective-permute-done.9.before_ref
  77.1 1.6 %collective-permute-start.16 = (f32[1,120,512]{2,1,0:T(8,128)S(1)}, f32[1,120,512]{2,1,0:T(8,128)S(1)}, u32[]{:S(2)}, u32[]{:S(2)}) collective-permute-start(f32[1,120,512]{2,1,0:T(8,128)S(1)} %get-tuple-element.109.refs_0_), channel_id=1, source_target_pairs={{0,16},{4,20},{8,24},{12,28},{16,0},{20,4},{24,8},{28,12},{1,17},{... | collective-permute-start | bytes 737288 | tf_op jit(solution)/shard_map/ppermute | solution.py:26
  78.7 0.0 collective-permute-done.11.refs_0_
  78.7 0.0 collective-permute-done.12.refs_1_
  78.7 0.0 collective-permute-done.13.refs_2_
  78.7 1.4 %collective-permute-start.17 = (f32[1,120,512]{2,1,0:T(8,128)S(1)}, f32[1,120,512]{2,1,0:T(8,128)S(1)}, u32[]{:S(2)}, u32[]{:S(2)}) collective-permute-start(f32[1,120,512]{2,1,0:T(8,128)S(1)} %get-tuple-element.116.refs_0_), channel_id=1, source_target_pairs={{0,16},{4,20},{8,24},{12,28},{16,0},{20,4},{24,8},{28,12},{1,17},{... | collective-permute-start | bytes 737288 | tf_op jit(solution)/shard_map/ppermute | solution.py:26
  80.1 0.0 copy-done
  80.1 1.4 %smooth_y.1 = (f32[8,256,512]{2,1,0:T(8,128)}, f32[8,256,512]{2,1,0:T(8,128)}) custom-call(f32[2,64,512]{2,1,0:T(8,128)S(1)} %collective-permute-done.9.before_ref, f32[2,256,512]{2,1,0:T(8,128)S(1)} %bitcast.12, f32[2,64,512]{2,1,0:T(8,128)S(1)} %collective-permute-done.10.after_ref, f32[8,256,512]{2,1,0:T(8,128)S(1)} %copy-done), custom_call_target="tpu_custom_call" | custom-call | flops 9437184 | bytes 4718592 | tf_op jit(solution)/shard_map/smooth_y/pallas_call | solution.py:395
  81.6 2.5 %finish_short.1 = (f32[8,256,512]{2,1,0:T(8,128)}, f32[8,256,512]{2,1,0:T(8,128)}) custom-call(f32[4,256,512]{2,1,0:T(8,128)S(1)} %get-tuple-element.87.whole_ref, f32[4,8,512]{2,1,0:T(8,128)S(1)} %collective-permute-done.11.refs_0_, f32[4,8,512]{2,1,0:T(8,128)S(1)} %collective-permute-done.12.refs_1_, ...), custom_call_target="tpu_custom_call", output_to_operand_aliasing={{0}: (5, {}), {1}: (6, {})} | custom-call | flops 17170432 | bytes 8585216 | tf_op jit(solution)/shard_map/finish_short/pallas_call | solution.py:395
  84.0 0.0 collective-permute-done.15.refs_1_
  84.0 1.3 %finish.2 = (f32[16,128,512]{2,1,0:T(8,128)}, f32[16,128,512]{2,1,0:T(8,128)}) custom-call(f32[2,120,512]{2,1,0:T(8,128)S(1)} %smooth_yx.3.refs_0_, f32[2,120,512]{2,1,0:T(8,128)S(1)} %collective-permute-done.15.refs_1_, f32[16,128,512]{2,1,0:T(8,128)S(1)} %bitcast.8, f32[16,128,512]{2,1,0:T(8,128)} %bitcast.13, ...), custom_call_target="tpu_custom_call", output_to_operand_aliasing={{0}: (3, {}), {1}: (4, {})} | custom-call | flops 5111808 | bytes 2555904 | tf_op jit(solution)/shard_map/finish/pallas_call | solution.py:395
  85.3 0.8 collective-permute-done.16.refs_1_
  86.1 1.0 %finish.3 = (f32[16,128,512]{2,1,0:T(8,128)}, f32[16,128,512]{2,1,0:T(8,128)}) custom-call(f32[1,120,512]{2,1,0:T(8,128)S(1)} %get-tuple-element.109.refs_0_, f32[1,120,512]{2,1,0:T(8,128)S(1)} %collective-permute-done.16.refs_1_, f32[16,128,512]{2,1,0:T(8,128)S(1)} %bitcast.9, ...), custom_call_target="tpu_custom_call", output_to_operand_aliasing={{0}: (3, {}), {1}: (4, {})} | custom-call | flops 2555904 | bytes 1277952 | tf_op jit(solution)/shard_map/finish/pallas_call | solution.py:395
  87.1 2.8 %collective-permute-done.17.refs_1_ = f32[1,120,512]{2,1,0:T(8,128)S(1)} collective-permute-done((f32[1,120,512]{2,1,0:T(8,128)S(1)}, f32[1,120,512]{2,1,0:T(8,128)S(1)}, u32[]{:S(2)}, u32[]{:S(2)}) %collective-permute-start.17) | collective-permute-done | bytes 245792 | tf_op jit(solution)/shard_map/ppermute | solution.py:26
  90.0 1.0 %finish_last.1 = (f32[16,128,512]{2,1,0:T(8,128)}, f32[16,128,512]{2,1,0:T(8,128)}) custom-call(f32[1,120,512]{2,1,0:T(8,128)S(1)} %get-tuple-element.116.refs_0_, f32[1,120,512]{2,1,0:T(8,128)S(1)} %collective-permute-done.17.refs_1_, f32[16,128,512]{2,1,0:T(8,128)S(1)} %bitcast.10, ...), custom_call_target="tpu_custom_call", output_to_operand_aliasing={{0}: (3, {}), {1}: (4, {})} | custom-call | tf_op jit(solution)/shard_map/finish_last/pallas_call | solution.py:395
  (1 shorter events, 0.0 us)
Async XLA Ops:
  1.9 15.1 %collective-permute-start.3 = (f32[2,120,512]{2,1,0:T(8,128)S(1)}, f32[2,120,512]{2,1,0:T(8,128)S(1)}, u32[]{:S(2)}, u32[]{:S(2)}) collective-permute-start(f32[2,120,512]{2,1,0:T(8,128)S(1)} %pair_x.1.refs_0_), channel_id=1, source_target_pairs={{0,16},{4,20},{8,24},{12,28},{16,0},{20,4},{24,8},{28,12},{1,17},{... | collective-permute-start | bytes 1474568 | tf_op jit(solution)/shard_map/ppermute | solution.py:26
  6.9 20.4 %collective-permute-start = (f32[2,120,512]{2,1,0:T(8,128)S(1)}, f32[2,120,512]{2,1,0:T(8,128)S(1)}, u32[]{:S(2)}, u32[]{:S(2)}) collective-permute-start(f32[2,120,512]{2,1,0:T(8,128)S(1)} %smooth_x.1.refs_0_), channel_id=1, source_target_pairs={{0,16},{4,20},{8,24},{12,28},{16,0},{20,4},{24,8},{28,12},{1,17},{... | collective-permute-start | bytes 1474568 | tf_op jit(solution)/shard_map/ppermute | solution.py:26
  8.0 11.4 %collective-permute-start.1 = (f32[2,64,512]{2,1,0:T(8,128)S(1)}, f32[2,64,512]{2,1,0:T(8,128)S(1)}, u32[]{:S(2)}, u32[]{:S(2)}) collective-permute-start(f32[2,64,512]{2,1,0:T(8,128)S(1)} %get-tuple-element.127), channel_id=1, source_target_pairs={{0,1},{1,2},{2,3},{3,0},{4,5},{5,6},{6,7},{7,4},{8,9},{9,10},{10,1... | collective-permute-start | bytes 786440 | tf_op jit(solution)/shard_map/ppermute | solution.py:26
  10.1 12.8 %collective-permute-start.2 = (f32[2,64,512]{2,1,0:T(8,128)S(1)}, f32[2,64,512]{2,1,0:T(8,128)S(1)}, u32[]{:S(2)}, u32[]{:S(2)}) collective-permute-start(f32[2,64,512]{2,1,0:T(8,128)S(1)} %get-tuple-element.126), channel_id=1, source_target_pairs={{0,3},{1,0},{2,1},{3,2},{4,7},{5,4},{6,5},{7,6},{8,11},{9,8},{10,9... | collective-permute-start | bytes 786440 | tf_op jit(solution)/shard_map/ppermute | solution.py:26
  25.7 32.5 %collective-permute-start.7 = (f32[233,8,128]{2,1,0:T(8,128)S(1)}, f32[233,8,128]{2,1,0:T(8,128)S(1)}, u32[]{:S(2)}, u32[]{:S(2)}) collective-permute-start(f32[233,8,128]{2,1,0:T(8,128)S(1)} %smooth_yx_short.2.refs_0_), channel_id=1, source_target_pairs={{0,16},{4,20},{8,24},{12,28},{16,0},{20,4},{24,8},{28,12},{1,17},{... | collective-permute-start | bytes 2863112 | tf_op jit(solution)/shard_map/ppermute | solution.py:26
  29.0 11.7 %collective-permute-start.4 = (f32[2,64,512]{2,1,0:T(8,128)S(1)}, f32[2,64,512]{2,1,0:T(8,128)S(1)}, u32[]{:S(2)}, u32[]{:S(2)}) collective-permute-start(f32[2,64,512]{2,1,0:T(8,128)S(1)} %get-tuple-element.125), channel_id=1, source_target_pairs={{0,1},{1,2},{2,3},{3,0},{4,5},{5,6},{6,7},{7,4},{8,9},{9,10},{10,1... | collective-permute-start | bytes 786440 | tf_op jit(solution)/shard_map/ppermute | solution.py:26
  30.3 13.2 %collective-permute-start.5 = (f32[2,64,512]{2,1,0:T(8,128)S(1)}, f32[2,64,512]{2,1,0:T(8,128)S(1)}, u32[]{:S(2)}, u32[]{:S(2)}) collective-permute-start(f32[2,64,512]{2,1,0:T(8,128)S(1)} %get-tuple-element.124), channel_id=1, source_target_pairs={{0,3},{1,0},{2,1},{3,2},{4,7},{5,4},{6,5},{7,6},{8,11},{9,8},{10,9... | collective-permute-start | bytes 786440 | tf_op jit(solution)/shard_map/ppermute | solution.py:26
  46.2 24.1 %collective-permute-start.6 = (f32[233,8,128]{2,1,0:T(8,128)S(1)}, f32[233,8,128]{2,1,0:T(8,128)S(1)}, u32[]{:S(2)}, u32[]{:S(2)}) collective-permute-start(f32[233,8,128]{2,1,0:T(8,128)S(1)} %smooth_yx_short.3.refs_0_), channel_id=1, source_target_pairs={{0,16},{4,20},{8,24},{12,28},{16,0},{20,4},{24,8},{28,12},{1,17},{... | collective-permute-start | bytes 2863112 | tf_op jit(solution)/shard_map/ppermute | solution.py:26
  47.1 11.0 %collective-permute-start.8 = (f32[2,64,512]{2,1,0:T(8,128)S(1)}, f32[2,64,512]{2,1,0:T(8,128)S(1)}, u32[]{:S(2)}, u32[]{:S(2)}) collective-permute-start(f32[2,64,512]{2,1,0:T(8,128)S(1)} %get-tuple-element.123), channel_id=1, source_target_pairs={{0,1},{1,2},{2,3},{3,0},{4,5},{5,6},{6,7},{7,4},{8,9},{9,10},{10,1... | collective-permute-start | bytes 786440 | tf_op jit(solution)/shard_map/ppermute | solution.py:26
  48.2 13.8 %collective-permute-start.14 = (f32[2,64,512]{2,1,0:T(8,128)S(1)}, f32[2,64,512]{2,1,0:T(8,128)S(1)}, u32[]{:S(2)}, u32[]{:S(2)}) collective-permute-start(f32[2,64,512]{2,1,0:T(8,128)S(1)} %get-tuple-element.122), channel_id=1, source_target_pairs={{0,3},{1,0},{2,1},{3,2},{4,7},{5,4},{6,5},{7,6},{8,11},{9,8},{10,9... | collective-permute-start | bytes 786440 | tf_op jit(solution)/shard_map/ppermute | solution.py:26
  58.2 15.7 %collective-permute-start.10 = (f32[2,64,512]{2,1,0:T(8,128)S(1)}, f32[2,64,512]{2,1,0:T(8,128)S(1)}, u32[]{:S(2)}, u32[]{:S(2)}) collective-permute-start(f32[2,64,512]{2,1,0:T(8,128)S(1)} %get-tuple-element.128), channel_id=1, source_target_pairs={{0,3},{1,0},{2,1},{3,2},{4,7},{5,4},{6,5},{7,6},{8,11},{9,8},{10,9... | collective-permute-start | bytes 786440 | tf_op jit(solution)/shard_map/ppermute | solution.py:26
  58.3 18.8 %collective-permute-start.9 = (f32[2,64,512]{2,1,0:T(8,128)S(1)}, f32[2,64,512]{2,1,0:T(8,128)S(1)}, u32[]{:S(2)}, u32[]{:S(2)}) collective-permute-start(f32[2,64,512]{2,1,0:T(8,128)S(1)} %get-tuple-element.129), channel_id=1, source_target_pairs={{0,1},{1,2},{2,3},{3,0},{4,5},{5,6},{6,7},{7,4},{8,9},{9,10},{10,1... | collective-permute-start | bytes 786440 | tf_op jit(solution)/shard_map/ppermute | solution.py:26
  63.9 20.1 %collective-permute-start.15 = (f32[2,120,512]{2,1,0:T(8,128)S(1)}, f32[2,120,512]{2,1,0:T(8,128)S(1)}, u32[]{:S(2)}, u32[]{:S(2)}) collective-permute-start(f32[2,120,512]{2,1,0:T(8,128)S(1)} %smooth_yx.3.refs_0_), channel_id=1, source_target_pairs={{0,16},{4,20},{8,24},{12,28},{16,0},{20,4},{24,8},{28,12},{1,17},{... | collective-permute-start | bytes 1474568 | tf_op jit(solution)/shard_map/ppermute | solution.py:26
  70.3 9.8 %copy-start = (f32[8,256,512]{2,1,0:T(8,128)S(1)}, f32[8,256,512]{2,1,0:T(8,128)}, u32[]{:S(2)}) copy-start(f32[8,256,512]{2,1,0:T(8,128)} %c_ref.9) | copy-start | bytes 12582916
  71.0 7.7 %collective-permute-start.11 = (f32[4,8,512]{2,1,0:T(8,128)S(1)}, f32[4,8,512]{2,1,0:T(8,128)S(1)}, u32[]{:S(2)}, u32[]{:S(2)}) collective-permute-start(f32[4,8,512]{2,1,0:T(8,128)S(1)} %get-tuple-element.82), channel_id=1, source_target_pairs={{0,1},{1,2},{2,3},{3,0},{4,5},{5,6},{6,7},{7,4},{8,9},{9,10},{10,1... | collective-permute-start | bytes 196616 | tf_op jit(solution)/shard_map/ppermute | solution.py:26
  71.8 6.9 %collective-permute-start.12 = (f32[4,8,512]{2,1,0:T(8,128)S(1)}, f32[4,8,512]{2,1,0:T(8,128)S(1)}, u32[]{:S(2)}, u32[]{:S(2)}) collective-permute-start(f32[4,8,512]{2,1,0:T(8,128)S(1)} %get-tuple-element.83), channel_id=1, source_target_pairs={{0,2},{1,3},{2,0},{3,1},{4,6},{5,7},{6,4},{7,5},{8,10},{9,11},{10,... | collective-permute-start | bytes 196616 | tf_op jit(solution)/shard_map/ppermute | solution.py:26
  73.9 4.8 %collective-permute-start.13 = (f32[4,8,512]{2,1,0:T(8,128)S(1)}, f32[4,8,512]{2,1,0:T(8,128)S(1)}, u32[]{:S(2)}, u32[]{:S(2)}) collective-permute-start(f32[4,8,512]{2,1,0:T(8,128)S(1)} %get-tuple-element.84), channel_id=1, source_target_pairs={{0,3},{1,0},{2,1},{3,2},{4,7},{5,4},{6,5},{7,6},{8,11},{9,8},{10,9... | collective-permute-start | bytes 196616 | tf_op jit(solution)/shard_map/ppermute | solution.py:26
  77.1 9.0 %collective-permute-start.16 = (f32[1,120,512]{2,1,0:T(8,128)S(1)}, f32[1,120,512]{2,1,0:T(8,128)S(1)}, u32[]{:S(2)}, u32[]{:S(2)}) collective-permute-start(f32[1,120,512]{2,1,0:T(8,128)S(1)} %get-tuple-element.109.refs_0_), channel_id=1, source_target_pairs={{0,16},{4,20},{8,24},{12,28},{16,0},{20,4},{24,8},{28,12},{1,17},{... | collective-permute-start | bytes 737288 | tf_op jit(solution)/shard_map/ppermute | solution.py:26
  78.7 11.2 %collective-permute-start.17 = (f32[1,120,512]{2,1,0:T(8,128)S(1)}, f32[1,120,512]{2,1,0:T(8,128)S(1)}, u32[]{:S(2)}, u32[]{:S(2)}) collective-permute-start(f32[1,120,512]{2,1,0:T(8,128)S(1)} %get-tuple-element.116.refs_0_), channel_id=1, source_target_pairs={{0,16},{4,20},{8,24},{12,28},{16,0},{20,4},{24,8},{28,12},{1,17},{... | collective-permute-start | bytes 737288 | tf_op jit(solution)/shard_map/ppermute | solution.py:26
where the time goes:
time: 91.3 us; the launch traced here: 91 us
  waiting for transfers between devices  36.3 us (40%)
  starting transfers between devices  28.9 us (32%)
  Pallas kernels  22.6 us (25%)
  local copies, waits for them, and re-layouts  2.38 us (3%)
    ppermute x18, waiting for transfers between devices, passed_along(): return lax.ppermute(x, axis, [(i, (i + by) % peers) for i in range(peers)])  36.3 us
    ppermute x18, starting transfers between devices, passed_along(): return lax.ppermute(x, axis, [(i, (i + by) % peers) for i in range(peers)])  28.9 us
    pallas_call x15, Pallas kernels, call(): pl.pallas_call(kernel, grid=(steps,) if steps else (), in_specs=in_specs,...  22.6 us
    slice x3, local copies, waits for them, and re-layouts, halo(): source[start:stop, :REACH]  2.38 us
  transfers between devices with their start and end apart: 18, of which 10 were waited for; matrix products, arithmetic and copies ran while one was open for 3% of the time, Pallas kernels for 22%

commit v1 on v0

--- a/solution.py
+++ b/solution.py
@@ -156,20 +156,32 @@
         store_packed(out_ref, unit, pair_sums(read_ref[unit]))
 
 
-def x_kernel(first, units_ref, out_ref, read_ref, matrix_ref, read_sems):
+def x_kernel(first, parts, edge_planes, units_ref, out_ref, top_ref, bottom_ref, read_ref, matrix_ref, read_sems, edge_sems):
     count = out_ref.shape[0]
 
     def read(unit):
         return pltpu.make_async_copy(units_ref.at[first + unit], read_ref.at[unit], read_sems.at[unit])
 
+    edges = []
+    for at, plane in enumerate(edge_planes):
+        top = units_ref.at[plane * parts, pl.ds(0, REACH)]
+        bottom = units_ref.at[(plane + 1) * parts - 1, pl.ds(UNIT_ROWS - REACH, REACH)]
+        edges.append(pltpu.make_async_copy(top, top_ref.at[at], edge_sems.at[at, 0]))
+        edges.append(pltpu.make_async_copy(bottom, bottom_ref.at[at], edge_sems.at[at, 1]))
+
     for unit in range(count):
         read(unit).start()
+    for edge in edges:
+        edge.start()
     fill_matrix(matrix_ref, x_taps())
 
     @pl.loop(0, count)
     def _(unit):
         read(unit).wait()
         store_packed(out_ref, unit, x_smoothed(read_ref[unit], matrix_ref[...]))
+
+    for edge in edges:
+        edge.wait()
 
 
 def extended_groups(before_ref, c_ref, after_ref, offset):
@@ -451,20 +463,23 @@
     lead, ready = lax.optimization_barrier((lead, units))
     lead_moved = along_gz(lead)
     first = FIRST_PLANES * parts - LEAD_UNITS
-    first_block = call(
-        functools.partial(x_kernel, LEAD_UNITS),
+    edge_planes = range(FIRST_PLANES, FIRST_PLANES + sum(size for size, _ in LATER_GROUPS[0]))
+    edges_shape = pltpu.VMEM((len(edge_planes), REACH, width), jnp.float32)
+    first_block, top, bottom = call(
+        functools.partial(x_kernel, LEAD_UNITS, parts, edge_planes),
         "smooth_x",
         0,
         [anywhere()],
-        [in_vmem()],
-        [pltpu.VMEM((first, short, width), jnp.float32)],
+        [in_vmem()] * 3,
+        [pltpu.VMEM((first, short, width), jnp.float32), edges_shape, edges_shape],
         [in_hbm(ready)],
         scratch=[
             pltpu.VMEM((first, UNIT_ROWS, width), jnp.float32),
             matrix,
             pltpu.SemaphoreType.DMA((first,)),
+            pltpu.SemaphoreType.DMA((len(edge_planes), 2)),
         ],
-    )[0]
+    )
     first_block, ready = lax.optimization_barrier((first_block, coarse_six))
     first_moved = along_gz(first_block)
     sums = call(
@@ -480,7 +495,7 @@
 
     later, short_sent = [], []
     start = FIRST_PLANES
-    near = halo(ready, start, start + sum(size for size, _ in LATER_GROUPS[0]))
+    near = (passed_along(bottom, "gy", 1), passed_along(top, "gy", -1))
     near, sums = lax.optimization_barrier((near, sums))
     for number, sizes in enumerate(LATER_GROUPS):
         offset = 0

time: 91.3 us -> 90.3 us (0.989)
  local copies, waits for them, and re-layouts: 2.38 us -> 1.31 us
    slice x3 -> x2, local copies, waits for them, and re-layouts: 2.38 us -> 1.31 us  [halo(): source[start:stop, :REACH]]
  transfers between devices with their start and end apart: 18 -> 18, of which waited for: 10 -> 11; matrix products, arithmetic and copies ran while one was open for 3% -> 1% of each run, Pallas kernels for 22% -> 23%
where the time goes in v1:
time: 90.3 us; the launch traced here: 90 us
  waiting for transfers between devices  35.6 us (39%)
  starting transfers between devices  29.6 us (33%)
  Pallas kernels  22.8 us (25%)
  local copies, waits for them, and re-layouts  1.31 us (1%)
    ppermute x18, waiting for transfers between devices, passed_along(): return lax.ppermute(x, axis, [(i, (i + by) % peers) for i in range(peers)])  35.6 us
    ppermute x18, starting transfers between devices, passed_along(): return lax.ppermute(x, axis, [(i, (i + by) % peers) for i in range(peers)])  29.6 us
    pallas_call x15, Pallas kernels, call(): pl.pallas_call(kernel, grid=(steps,) if steps else (), in_specs=in_specs,...  22.8 us
  transfers between devices with their start and end apart: 18, of which 11 were waited for; matrix products, arithmetic and copies ran while one was open for 1% of the time, Pallas kernels for 23%

profile of v1, /device:TPU:0, one launch (start us, length us, event | category | flops | bytes accessed | tf_op | source)
XLA Modules:
  0.0 90.0 jit_solution(1157383048987388293)
XLA Ops:
  0.6 1.3 %pair_x.1.refs_0_ = f32[2,120,512]{2,1,0:T(8,128)S(1)} custom-call(f32[16,128,512]{2,1,0:T(8,128)} %bitcast.6), custom_call_target="tpu_custom_call" | custom-call | tf_op jit(solution)/shard_map/pair_x/pallas_call | solution.py:407
  1.9 3.0 %collective-permute-start.3 = (f32[2,120,512]{2,1,0:T(8,128)S(1)}, f32[2,120,512]{2,1,0:T(8,128)S(1)}, u32[]{:S(2)}, u32[]{:S(2)}) collective-permute-start(f32[2,120,512]{2,1,0:T(8,128)S(1)} %pair_x.1.refs_0_), channel_id=1, source_target_pairs={{0,16},{4,20},{8,24},{12,28},{16,0},{20,4},{24,8},{28,12},{1,17},{... | collective-permute-start | bytes 1474568 | tf_op jit(solution)/shard_map/ppermute | solution.py:26
  5.0 2.1 %smooth_x.1 = (f32[2,120,512]{2,1,0:T(8,128)S(1)}, f32[2,64,512]{2,1,0:T(8,128)S(1)}, f32[2,64,512]{2,1,0:T(8,128)S(1)}) custom-call(f32[16,128,512]{2,1,0:T(8,128)} %bitcast.7), custom_call_target="tpu_custom_call" | custom-call | tf_op jit(solution)/shard_map/smooth_x/pallas_call | solution.py:407
  7.0 0.1 collective-permute-start
  7.1 2.1 %collective-permute-start.1 = (f32[2,64,512]{2,1,0:T(8,128)S(1)}, f32[2,64,512]{2,1,0:T(8,128)S(1)}, u32[]{:S(2)}, u32[]{:S(2)}) collective-permute-start(f32[2,64,512]{2,1,0:T(8,128)S(1)} %get-tuple-element.68), channel_id=1, source_target_pairs={{0,1},{1,2},{2,3},{3,0},{4,5},{5,6},{6,7},{7,4},{8,9},{9,10},{10,1... | collective-permute-start | bytes 786440 | tf_op jit(solution)/shard_map/ppermute | solution.py:26
  9.2 2.0 %collective-permute-start.2 = (f32[2,64,512]{2,1,0:T(8,128)S(1)}, f32[2,64,512]{2,1,0:T(8,128)S(1)}, u32[]{:S(2)}, u32[]{:S(2)}) collective-permute-start(f32[2,64,512]{2,1,0:T(8,128)S(1)} %get-tuple-element.69), channel_id=1, source_target_pairs={{0,3},{1,0},{2,1},{3,2},{4,7},{5,4},{6,5},{7,6},{8,11},{9,8},{10,9... | collective-permute-start | bytes 786440 | tf_op jit(solution)/shard_map/ppermute | solution.py:26
  11.2 5.8 %collective-permute-done.3.refs_1_ = f32[2,120,512]{2,1,0:T(8,128)S(1)} collective-permute-done((f32[2,120,512]{2,1,0:T(8,128)S(1)}, f32[2,120,512]{2,1,0:T(8,128)S(1)}, u32[]{:S(2)}, u32[]{:S(2)}) %collective-permute-start.3) | collective-permute-done | bytes 491552 | tf_op jit(solution)/shard_map/ppermute | solution.py:26
  17.0 1.1 %smooth_zx.1.refs_2_ = f32[4,128,512]{2,1,0:T(8,128)S(1)} custom-call(f32[2,120,512]{2,1,0:T(8,128)S(1)} %pair_x.1.refs_0_, f32[2,120,512]{2,1,0:T(8,128)S(1)} %collective-permute-done.3.refs_1_), custom_call_target="tpu_custom_call" | custom-call | flops 3014656 | bytes 1507328 | tf_op jit(solution)/shard_map/smooth_zx/pallas_call | solution.py:407
  18.1 0.3 collective-permute-done.1.before_ref
  18.4 3.5 %collective-permute-done.2.after_ref = f32[2,64,512]{2,1,0:T(8,128)S(1)} collective-permute-done((f32[2,64,512]{2,1,0:T(8,128)S(1)}, f32[2,64,512]{2,1,0:T(8,128)S(1)}, u32[]{:S(2)}, u32[]{:S(2)}) %collective-permute-start.2) | collective-permute-done | bytes 262176 | tf_op jit(solution)/shard_map/ppermute | solution.py:26
  22.0 2.7 %smooth_yx_short.2.refs_0_ = f32[233,8,128]{2,1,0:T(8,128)S(1)} custom-call(f32[2,64,512]{2,1,0:T(8,128)S(1)} %collective-permute-done.1.before_ref, f32[8,256,512]{2,1,0:T(8,128)} %c_ref.9, f32[2,64,512]{2,1,0:T(8,128)S(1)} %collective-permute-done.2.after_ref), custom_call_target="tpu_custom_call" | custom-call | flops 6963200 | bytes 3481600 | tf_op jit(solution)/shard_map/smooth_yx_short/pallas_call | solution.py:407
  24.7 1.6 %collective-permute-start.7 = (f32[233,8,128]{2,1,0:T(8,128)S(1)}, f32[233,8,128]{2,1,0:T(8,128)S(1)}, u32[]{:S(2)}, u32[]{:S(2)}) collective-permute-start(f32[233,8,128]{2,1,0:T(8,128)S(1)} %smooth_yx_short.2.refs_0_), channel_id=1, source_target_pairs={{0,16},{4,20},{8,24},{12,28},{16,0},{20,4},{24,8},{28,12},{1,17},{... | collective-permute-start | bytes 2863112 | tf_op jit(solution)/shard_map/ppermute | solution.py:26
  26.3 0.4 collective-permute-done.refs_1_
  26.7 0.5 smooth_z.1
  27.2 1.3 %fusion = (f32[2,64,512]{2,1,0:T(8,128)S(1)}, f32[2,64,512]{2,1,0:T(8,128)S(1)}, f32[2,64,512]{2,1,0:T(8,128)S(1)}, f32[2,64,512]{2,1,0:T(8,128)S(1)}) fusion(f32[8,256,512]{2,1,0:T(8,128)} %c_ref.9), kind=kLoop, calls=%fused_computation | loop fusion | bytes 2097152 | tf_op jit(solution)/shard_map/slice | solution.py:449
  28.4 1.8 %collective-permute-start.4 = (f32[2,64,512]{2,1,0:T(8,128)S(1)}, f32[2,64,512]{2,1,0:T(8,128)S(1)}, u32[]{:S(2)}, u32[]{:S(2)}) collective-permute-start(f32[2,64,512]{2,1,0:T(8,128)S(1)} %get-tuple-element.131), channel_id=1, source_target_pairs={{0,1},{1,2},{2,3},{3,0},{4,5},{5,6},{6,7},{7,4},{8,9},{9,10},{10,1... | collective-permute-start | bytes 786440 | tf_op jit(solution)/shard_map/ppermute | solution.py:26
  30.3 3.2 %collective-permute-start.5 = (f32[2,64,512]{2,1,0:T(8,128)S(1)}, f32[2,64,512]{2,1,0:T(8,128)S(1)}, u32[]{:S(2)}, u32[]{:S(2)}) collective-permute-start(f32[2,64,512]{2,1,0:T(8,128)S(1)} %get-tuple-element.130), channel_id=1, source_target_pairs={{0,3},{1,0},{2,1},{3,2},{4,7},{5,4},{6,5},{7,6},{8,11},{9,8},{10,9... | collective-permute-start | bytes 786440 | tf_op jit(solution)/shard_map/ppermute | solution.py:26
  33.5 7.1 %collective-permute-done.4.before_ref = f32[2,64,512]{2,1,0:T(8,128)S(1)} collective-permute-done((f32[2,64,512]{2,1,0:T(8,128)S(1)}, f32[2,64,512]{2,1,0:T(8,128)S(1)}, u32[]{:S(2)}, u32[]{:S(2)}) %collective-permute-start.4) | collective-permute-done | bytes 262176 | tf_op jit(solution)/shard_map/ppermute | solution.py:26
  40.7 2.2 %collective-permute-done.5.after_ref = f32[2,64,512]{2,1,0:T(8,128)S(1)} collective-permute-done((f32[2,64,512]{2,1,0:T(8,128)S(1)}, f32[2,64,512]{2,1,0:T(8,128)S(1)}, u32[]{:S(2)}, u32[]{:S(2)}) %collective-permute-start.5) | collective-permute-done | bytes 262176 | tf_op jit(solution)/shard_map/ppermute | solution.py:26
  42.8 2.7 %smooth_yx_short.3.refs_0_ = f32[233,8,128]{2,1,0:T(8,128)S(1)} custom-call(f32[2,64,512]{2,1,0:T(8,128)S(1)} %collective-permute-done.4.before_ref, f32[8,256,512]{2,1,0:T(8,128)} %c_ref.9, f32[2,64,512]{2,1,0:T(8,128)S(1)} %collective-permute-done.5.after_ref), custom_call_target="tpu_custom_call" | custom-call | flops 6963200 | bytes 3481600 | tf_op jit(solution)/shard_map/smooth_yx_short/pallas_call | solution.py:407
  45.5 1.6 %collective-permute-start.6 = (f32[233,8,128]{2,1,0:T(8,128)S(1)}, f32[233,8,128]{2,1,0:T(8,128)S(1)}, u32[]{:S(2)}, u32[]{:S(2)}) collective-permute-start(f32[233,8,128]{2,1,0:T(8,128)S(1)} %smooth_yx_short.3.refs_0_), channel_id=1, source_target_pairs={{0,16},{4,20},{8,24},{12,28},{16,0},{20,4},{24,8},{28,12},{1,17},{... | collective-permute-start | bytes 2863112 | tf_op jit(solution)/shard_map/ppermute | solution.py:26
  47.1 1.1 %collective-permute-start.8 = (f32[2,64,512]{2,1,0:T(8,128)S(1)}, f32[2,64,512]{2,1,0:T(8,128)S(1)}, u32[]{:S(2)}, u32[]{:S(2)}) collective-permute-start(f32[2,64,512]{2,1,0:T(8,128)S(1)} %get-tuple-element.129), channel_id=1, source_target_pairs={{0,1},{1,2},{2,3},{3,0},{4,5},{5,6},{6,7},{7,4},{8,9},{9,10},{10,1... | collective-permute-start | bytes 786440 | tf_op jit(solution)/shard_map/ppermute | solution.py:26
  48.2 2.7 %collective-permute-start.14 = (f32[2,64,512]{2,1,0:T(8,128)S(1)}, f32[2,64,512]{2,1,0:T(8,128)S(1)}, u32[]{:S(2)}, u32[]{:S(2)}) collective-permute-start(f32[2,64,512]{2,1,0:T(8,128)S(1)} %get-tuple-element.128), channel_id=1, source_target_pairs={{0,3},{1,0},{2,1},{3,2},{4,7},{5,4},{6,5},{7,6},{8,11},{9,8},{10,9... | collective-permute-start | bytes 786440 | tf_op jit(solution)/shard_map/ppermute | solution.py:26
  50.9 7.2 %collective-permute-done.8.before_ref = f32[2,64,512]{2,1,0:T(8,128)S(1)} collective-permute-done((f32[2,64,512]{2,1,0:T(8,128)S(1)}, f32[2,64,512]{2,1,0:T(8,128)S(1)}, u32[]{:S(2)}, u32[]{:S(2)}) %collective-permute-start.8) | collective-permute-done | bytes 262176 | tf_op jit(solution)/shard_map/ppermute | solution.py:26
  58.1 0.0 collective-permute-done.7.refs_1_
  58.2 0.1 collective-permute-start.10
  58.3 2.0 %collective-permute-start.9 = (f32[2,64,512]{2,1,0:T(8,128)S(1)}, f32[2,64,512]{2,1,0:T(8,128)S(1)}, u32[]{:S(2)}, u32[]{:S(2)}) collective-permute-start(f32[2,64,512]{2,1,0:T(8,128)S(1)} %get-tuple-element.133), channel_id=1, source_target_pairs={{0,1},{1,2},{2,3},{3,0},{4,5},{5,6},{6,7},{7,4},{8,9},{9,10},{10,1... | collective-permute-start | bytes 786440 | tf_op jit(solution)/shard_map/ppermute | solution.py:26
  60.3 1.7 %collective-permute-done.14.after_ref = f32[2,64,512]{2,1,0:T(8,128)S(1)} collective-permute-done((f32[2,64,512]{2,1,0:T(8,128)S(1)}, f32[2,64,512]{2,1,0:T(8,128)S(1)}, u32[]{:S(2)}, u32[]{:S(2)}) %collective-permute-start.14) | collective-permute-done | bytes 262176 | tf_op jit(solution)/shard_map/ppermute | solution.py:26
  62.0 1.9 %smooth_yx.3.refs_0_ = f32[2,120,512]{2,1,0:T(8,128)S(1)} custom-call(f32[2,64,512]{2,1,0:T(8,128)S(1)} %collective-permute-done.8.before_ref, f32[8,256,512]{2,1,0:T(8,128)} %c_ref.9, f32[2,64,512]{2,1,0:T(8,128)S(1)} %collective-permute-done.14.after_ref), custom_call_target="tpu_custom_call" | custom-call | flops 2555904 | bytes 1277952 | tf_op jit(solution)/shard_map/smooth_yx/pallas_call | solution.py:407
  63.9 0.5 collective-permute-start.15
  64.5 0.7 smooth_z_short.2
  65.1 4.5 %collective-permute-done.6.refs_1_ = f32[233,8,128]{2,1,0:T(8,128)S(1)} collective-permute-done((f32[233,8,128]{2,1,0:T(8,128)S(1)}, f32[233,8,128]{2,1,0:T(8,128)S(1)}, u32[]{:S(2)}, u32[]{:S(2)}) %collective-permute-start.6) | collective-permute-done | bytes 954400 | tf_op jit(solution)/shard_map/ppermute | solution.py:26
  69.7 0.0 copy-start
  69.7 0.7 smooth_z_short.3
  70.4 1.2 %collective-permute-start.11 = (f32[4,8,512]{2,1,0:T(8,128)S(1)}, f32[4,8,512]{2,1,0:T(8,128)S(1)}, u32[]{:S(2)}, u32[]{:S(2)}) collective-permute-start(f32[4,8,512]{2,1,0:T(8,128)S(1)} %get-tuple-element.88), channel_id=1, source_target_pairs={{0,1},{1,2},{2,3},{3,0},{4,5},{5,6},{6,7},{7,4},{8,9},{9,10},{10,1... | collective-permute-start | bytes 196616 | tf_op jit(solution)/shard_map/ppermute | solution.py:26
  71.6 2.3 %collective-permute-start.12 = (f32[4,8,512]{2,1,0:T(8,128)S(1)}, f32[4,8,512]{2,1,0:T(8,128)S(1)}, u32[]{:S(2)}, u32[]{:S(2)}) collective-permute-start(f32[4,8,512]{2,1,0:T(8,128)S(1)} %get-tuple-element.89), channel_id=1, source_target_pairs={{0,2},{1,3},{2,0},{3,1},{4,6},{5,7},{6,4},{7,5},{8,10},{9,11},{10,... | collective-permute-start | bytes 196616 | tf_op jit(solution)/shard_map/ppermute | solution.py:26
  73.9 0.0 collective-permute-done.10.after_ref
  73.9 1.3 %collective-permute-start.13 = (f32[4,8,512]{2,1,0:T(8,128)S(1)}, f32[4,8,512]{2,1,0:T(8,128)S(1)}, u32[]{:S(2)}, u32[]{:S(2)}) collective-permute-start(f32[4,8,512]{2,1,0:T(8,128)S(1)} %get-tuple-element.90), channel_id=1, source_target_pairs={{0,3},{1,0},{2,1},{3,2},{4,7},{5,4},{6,5},{7,6},{8,11},{9,8},{10,9... | collective-permute-start | bytes 196616 | tf_op jit(solution)/shard_map/ppermute | solution.py:26
  75.2 1.9 %smooth_yx.2 = (f32[1,120,512]{2,1,0:T(8,128)S(1)}, f32[1,120,512]{2,1,0:T(8,128)S(1)}) custom-call(f32[2,64,512]{2,1,0:T(8,128)S(1)} %collective-permute-done.8.before_ref, f32[8,256,512]{2,1,0:T(8,128)} %c_ref.9, f32[2,64,512]{2,1,0:T(8,128)S(1)} %collective-permute-done.14.after_ref), custom_call_target="tpu_custom_call" | custom-call | flops 2555904 | bytes 1277952 | tf_op jit(solution)/shard_map/smooth_yx/pallas_call | solution.py:407
  77.1 0.0 collective-permute-done.9.before_ref
  77.1 1.6 %collective-permute-start.16 = (f32[1,120,512]{2,1,0:T(8,128)S(1)}, f32[1,120,512]{2,1,0:T(8,128)S(1)}, u32[]{:S(2)}, u32[]{:S(2)}) collective-permute-start(f32[1,120,512]{2,1,0:T(8,128)S(1)} %get-tuple-element.115.refs_0_), channel_id=1, source_target_pairs={{0,16},{4,20},{8,24},{12,28},{16,0},{20,4},{24,8},{28,12},{1,17},{... | collective-permute-start | bytes 737288 | tf_op jit(solution)/shard_map/ppermute | solution.py:26
  78.7 0.0 collective-permute-done.11.refs_0_
  78.7 0.0 collective-permute-done.12.refs_1_
  78.7 0.0 collective-permute-done.13.refs_2_
  78.7 1.3 %collective-permute-start.17 = (f32[1,120,512]{2,1,0:T(8,128)S(1)}, f32[1,120,512]{2,1,0:T(8,128)S(1)}, u32[]{:S(2)}, u32[]{:S(2)}) collective-permute-start(f32[1,120,512]{2,1,0:T(8,128)S(1)} %get-tuple-element.122.refs_0_), channel_id=1, source_target_pairs={{0,16},{4,20},{8,24},{12,28},{16,0},{20,4},{24,8},{28,12},{1,17},{... | collective-permute-start | bytes 737288 | tf_op jit(solution)/shard_map/ppermute | solution.py:26
  80.1 0.0 copy-done
  80.1 1.4 %smooth_y.1 = (f32[8,256,512]{2,1,0:T(8,128)}, f32[8,256,512]{2,1,0:T(8,128)}) custom-call(f32[2,64,512]{2,1,0:T(8,128)S(1)} %collective-permute-done.9.before_ref, f32[2,256,512]{2,1,0:T(8,128)S(1)} %bitcast.12, f32[2,64,512]{2,1,0:T(8,128)S(1)} %collective-permute-done.10.after_ref, f32[8,256,512]{2,1,0:T(8,128)S(1)} %copy-done), custom_call_target="tpu_custom_call" | custom-call | flops 9437184 | bytes 4718592 | tf_op jit(solution)/shard_map/smooth_y/pallas_call | solution.py:407
  81.5 2.5 %finish_short.1 = (f32[8,256,512]{2,1,0:T(8,128)}, f32[8,256,512]{2,1,0:T(8,128)}) custom-call(f32[4,256,512]{2,1,0:T(8,128)S(1)} %get-tuple-element.93.whole_ref, f32[4,8,512]{2,1,0:T(8,128)S(1)} %collective-permute-done.11.refs_0_, f32[4,8,512]{2,1,0:T(8,128)S(1)} %collective-permute-done.12.refs_1_, ...), custom_call_target="tpu_custom_call", output_to_operand_aliasing={{0}: (5, {}), {1}: (6, {})} | custom-call | flops 17170432 | bytes 8585216 | tf_op jit(solution)/shard_map/finish_short/pallas_call | solution.py:407
  84.0 0.0 collective-permute-done.15.refs_1_
  84.0 1.3 %finish.2 = (f32[16,128,512]{2,1,0:T(8,128)}, f32[16,128,512]{2,1,0:T(8,128)}) custom-call(f32[2,120,512]{2,1,0:T(8,128)S(1)} %smooth_yx.3.refs_0_, f32[2,120,512]{2,1,0:T(8,128)S(1)} %collective-permute-done.15.refs_1_, f32[16,128,512]{2,1,0:T(8,128)S(1)} %bitcast.8, f32[16,128,512]{2,1,0:T(8,128)} %bitcast.13, ...), custom_call_target="tpu_custom_call", output_to_operand_aliasing={{0}: (3, {}), {1}: (4, {})} | custom-call | flops 5111808 | bytes 2555904 | tf_op jit(solution)/shard_map/finish/pallas_call | solution.py:407
  85.3 0.9 collective-permute-done.16.refs_1_
  86.1 1.0 %finish.3 = (f32[16,128,512]{2,1,0:T(8,128)}, f32[16,128,512]{2,1,0:T(8,128)}) custom-call(f32[1,120,512]{2,1,0:T(8,128)S(1)} %get-tuple-element.115.refs_0_, f32[1,120,512]{2,1,0:T(8,128)S(1)} %collective-permute-done.16.refs_1_, f32[16,128,512]{2,1,0:T(8,128)S(1)} %bitcast.9, ...), custom_call_target="tpu_custom_call", output_to_operand_aliasing={{0}: (3, {}), {1}: (4, {})} | custom-call | flops 2555904 | bytes 1277952 | tf_op jit(solution)/shard_map/finish/pallas_call | solution.py:407
  87.1 1.9 %collective-permute-done.17.refs_1_ = f32[1,120,512]{2,1,0:T(8,128)S(1)} collective-permute-done((f32[1,120,512]{2,1,0:T(8,128)S(1)}, f32[1,120,512]{2,1,0:T(8,128)S(1)}, u32[]{:S(2)}, u32[]{:S(2)}) %collective-permute-start.17) | collective-permute-done | bytes 245792 | tf_op jit(solution)/shard_map/ppermute | solution.py:26
  89.0 1.0 %finish_last.1 = (f32[16,128,512]{2,1,0:T(8,128)}, f32[16,128,512]{2,1,0:T(8,128)}) custom-call(f32[1,120,512]{2,1,0:T(8,128)S(1)} %get-tuple-element.122.refs_0_, f32[1,120,512]{2,1,0:T(8,128)S(1)} %collective-permute-done.17.refs_1_, f32[16,128,512]{2,1,0:T(8,128)S(1)} %bitcast.10, ...), custom_call_target="tpu_custom_call", output_to_operand_aliasing={{0}: (3, {}), {1}: (4, {})} | custom-call | tf_op jit(solution)/shard_map/finish_last/pallas_call | solution.py:407
  (1 shorter events, 0.0 us)
Async XLA Ops:
  1.9 15.1 %collective-permute-start.3 = (f32[2,120,512]{2,1,0:T(8,128)S(1)}, f32[2,120,512]{2,1,0:T(8,128)S(1)}, u32[]{:S(2)}, u32[]{:S(2)}) collective-permute-start(f32[2,120,512]{2,1,0:T(8,128)S(1)} %pair_x.1.refs_0_), channel_id=1, source_target_pairs={{0,16},{4,20},{8,24},{12,28},{16,0},{20,4},{24,8},{28,12},{1,17},{... | collective-permute-start | bytes 1474568 | tf_op jit(solution)/shard_map/ppermute | solution.py:26
  7.0 19.7 %collective-permute-start = (f32[2,120,512]{2,1,0:T(8,128)S(1)}, f32[2,120,512]{2,1,0:T(8,128)S(1)}, u32[]{:S(2)}, u32[]{:S(2)}) collective-permute-start(f32[2,120,512]{2,1,0:T(8,128)S(1)} %get-tuple-element.67.refs_0_), channel_id=1, source_target_pairs={{0,16},{4,20},{8,24},{12,28},{16,0},{20,4},{24,8},{28,12},{1,17},{... | collective-permute-start | bytes 1474568 | tf_op jit(solution)/shard_map/ppermute | solution.py:26
  7.1 11.3 %collective-permute-start.1 = (f32[2,64,512]{2,1,0:T(8,128)S(1)}, f32[2,64,512]{2,1,0:T(8,128)S(1)}, u32[]{:S(2)}, u32[]{:S(2)}) collective-permute-start(f32[2,64,512]{2,1,0:T(8,128)S(1)} %get-tuple-element.68), channel_id=1, source_target_pairs={{0,1},{1,2},{2,3},{3,0},{4,5},{5,6},{6,7},{7,4},{8,9},{9,10},{10,1... | collective-permute-start | bytes 786440 | tf_op jit(solution)/shard_map/ppermute | solution.py:26
  9.2 12.8 %collective-permute-start.2 = (f32[2,64,512]{2,1,0:T(8,128)S(1)}, f32[2,64,512]{2,1,0:T(8,128)S(1)}, u32[]{:S(2)}, u32[]{:S(2)}) collective-permute-start(f32[2,64,512]{2,1,0:T(8,128)S(1)} %get-tuple-element.69), channel_id=1, source_target_pairs={{0,3},{1,0},{2,1},{3,2},{4,7},{5,4},{6,5},{7,6},{8,11},{9,8},{10,9... | collective-permute-start | bytes 786440 | tf_op jit(solution)/shard_map/ppermute | solution.py:26
  24.7 33.4 %collective-permute-start.7 = (f32[233,8,128]{2,1,0:T(8,128)S(1)}, f32[233,8,128]{2,1,0:T(8,128)S(1)}, u32[]{:S(2)}, u32[]{:S(2)}) collective-permute-start(f32[233,8,128]{2,1,0:T(8,128)S(1)} %smooth_yx_short.2.refs_0_), channel_id=1, source_target_pairs={{0,16},{4,20},{8,24},{12,28},{16,0},{20,4},{24,8},{28,12},{1,17},{... | collective-permute-start | bytes 2863112 | tf_op jit(solution)/shard_map/ppermute | solution.py:26
  28.4 12.2 %collective-permute-start.4 = (f32[2,64,512]{2,1,0:T(8,128)S(1)}, f32[2,64,512]{2,1,0:T(8,128)S(1)}, u32[]{:S(2)}, u32[]{:S(2)}) collective-permute-start(f32[2,64,512]{2,1,0:T(8,128)S(1)} %get-tuple-element.131), channel_id=1, source_target_pairs={{0,1},{1,2},{2,3},{3,0},{4,5},{5,6},{6,7},{7,4},{8,9},{9,10},{10,1... | collective-permute-start | bytes 786440 | tf_op jit(solution)/shard_map/ppermute | solution.py:26
  30.3 12.5 %collective-permute-start.5 = (f32[2,64,512]{2,1,0:T(8,128)S(1)}, f32[2,64,512]{2,1,0:T(8,128)S(1)}, u32[]{:S(2)}, u32[]{:S(2)}) collective-permute-start(f32[2,64,512]{2,1,0:T(8,128)S(1)} %get-tuple-element.130), channel_id=1, source_target_pairs={{0,3},{1,0},{2,1},{3,2},{4,7},{5,4},{6,5},{7,6},{8,11},{9,8},{10,9... | collective-permute-start | bytes 786440 | tf_op jit(solution)/shard_map/ppermute | solution.py:26
  45.5 24.1 %collective-permute-start.6 = (f32[233,8,128]{2,1,0:T(8,128)S(1)}, f32[233,8,128]{2,1,0:T(8,128)S(1)}, u32[]{:S(2)}, u32[]{:S(2)}) collective-permute-start(f32[233,8,128]{2,1,0:T(8,128)S(1)} %smooth_yx_short.3.refs_0_), channel_id=1, source_target_pairs={{0,16},{4,20},{8,24},{12,28},{16,0},{20,4},{24,8},{28,12},{1,17},{... | collective-permute-start | bytes 2863112 | tf_op jit(solution)/shard_map/ppermute | solution.py:26
  47.1 11.0 %collective-permute-start.8 = (f32[2,64,512]{2,1,0:T(8,128)S(1)}, f32[2,64,512]{2,1,0:T(8,128)S(1)}, u32[]{:S(2)}, u32[]{:S(2)}) collective-permute-start(f32[2,64,512]{2,1,0:T(8,128)S(1)} %get-tuple-element.129), channel_id=1, source_target_pairs={{0,1},{1,2},{2,3},{3,0},{4,5},{5,6},{6,7},{7,4},{8,9},{9,10},{10,1... | collective-permute-start | bytes 786440 | tf_op jit(solution)/shard_map/ppermute | solution.py:26
  48.2 13.8 %collective-permute-start.14 = (f32[2,64,512]{2,1,0:T(8,128)S(1)}, f32[2,64,512]{2,1,0:T(8,128)S(1)}, u32[]{:S(2)}, u32[]{:S(2)}) collective-permute-start(f32[2,64,512]{2,1,0:T(8,128)S(1)} %get-tuple-element.128), channel_id=1, source_target_pairs={{0,3},{1,0},{2,1},{3,2},{4,7},{5,4},{6,5},{7,6},{8,11},{9,8},{10,9... | collective-permute-start | bytes 786440 | tf_op jit(solution)/shard_map/ppermute | solution.py:26
  58.2 15.7 %collective-permute-start.10 = (f32[2,64,512]{2,1,0:T(8,128)S(1)}, f32[2,64,512]{2,1,0:T(8,128)S(1)}, u32[]{:S(2)}, u32[]{:S(2)}) collective-permute-start(f32[2,64,512]{2,1,0:T(8,128)S(1)} %get-tuple-element.132), channel_id=1, source_target_pairs={{0,3},{1,0},{2,1},{3,2},{4,7},{5,4},{6,5},{7,6},{8,11},{9,8},{10,9... | collective-permute-start | bytes 786440 | tf_op jit(solution)/shard_map/ppermute | solution.py:26
  58.3 18.9 %collective-permute-start.9 = (f32[2,64,512]{2,1,0:T(8,128)S(1)}, f32[2,64,512]{2,1,0:T(8,128)S(1)}, u32[]{:S(2)}, u32[]{:S(2)}) collective-permute-start(f32[2,64,512]{2,1,0:T(8,128)S(1)} %get-tuple-element.133), channel_id=1, source_target_pairs={{0,1},{1,2},{2,3},{3,0},{4,5},{5,6},{6,7},{7,4},{8,9},{9,10},{10,1... | collective-permute-start | bytes 786440 | tf_op jit(solution)/shard_map/ppermute | solution.py:26
  63.9 20.0 %collective-permute-start.15 = (f32[2,120,512]{2,1,0:T(8,128)S(1)}, f32[2,120,512]{2,1,0:T(8,128)S(1)}, u32[]{:S(2)}, u32[]{:S(2)}) collective-permute-start(f32[2,120,512]{2,1,0:T(8,128)S(1)} %smooth_yx.3.refs_0_), channel_id=1, source_target_pairs={{0,16},{4,20},{8,24},{12,28},{16,0},{20,4},{24,8},{28,12},{1,17},{... | collective-permute-start | bytes 1474568 | tf_op jit(solution)/shard_map/ppermute | solution.py:26
  69.7 10.4 %copy-start = (f32[8,256,512]{2,1,0:T(8,128)S(1)}, f32[8,256,512]{2,1,0:T(8,128)}, u32[]{:S(2)}) copy-start(f32[8,256,512]{2,1,0:T(8,128)} %c_ref.9) | copy-start | bytes 12582916
  70.4 8.4 %collective-permute-start.11 = (f32[4,8,512]{2,1,0:T(8,128)S(1)}, f32[4,8,512]{2,1,0:T(8,128)S(1)}, u32[]{:S(2)}, u32[]{:S(2)}) collective-permute-start(f32[4,8,512]{2,1,0:T(8,128)S(1)} %get-tuple-element.88), channel_id=1, source_target_pairs={{0,1},{1,2},{2,3},{3,0},{4,5},{5,6},{6,7},{7,4},{8,9},{9,10},{10,1... | collective-permute-start | bytes 196616 | tf_op jit(solution)/shard_map/ppermute | solution.py:26
  71.6 7.2 %collective-permute-start.12 = (f32[4,8,512]{2,1,0:T(8,128)S(1)}, f32[4,8,512]{2,1,0:T(8,128)S(1)}, u32[]{:S(2)}, u32[]{:S(2)}) collective-permute-start(f32[4,8,512]{2,1,0:T(8,128)S(1)} %get-tuple-element.89), channel_id=1, source_target_pairs={{0,2},{1,3},{2,0},{3,1},{4,6},{5,7},{6,4},{7,5},{8,10},{9,11},{10,... | collective-permute-start | bytes 196616 | tf_op jit(solution)/shard_map/ppermute | solution.py:26
  73.9 4.9 %collective-permute-start.13 = (f32[4,8,512]{2,1,0:T(8,128)S(1)}, f32[4,8,512]{2,1,0:T(8,128)S(1)}, u32[]{:S(2)}, u32[]{:S(2)}) collective-permute-start(f32[4,8,512]{2,1,0:T(8,128)S(1)} %get-tuple-element.90), channel_id=1, source_target_pairs={{0,3},{1,0},{2,1},{3,2},{4,7},{5,4},{6,5},{7,6},{8,11},{9,8},{10,9... | collective-permute-start | bytes 196616 | tf_op jit(solution)/shard_map/ppermute | solution.py:26
  77.1 9.0 %collective-permute-start.16 = (f32[1,120,512]{2,1,0:T(8,128)S(1)}, f32[1,120,512]{2,1,0:T(8,128)S(1)}, u32[]{:S(2)}, u32[]{:S(2)}) collective-permute-start(f32[1,120,512]{2,1,0:T(8,128)S(1)} %get-tuple-element.115.refs_0_), channel_id=1, source_target_pairs={{0,16},{4,20},{8,24},{12,28},{16,0},{20,4},{24,8},{28,12},{1,17},{... | collective-permute-start | bytes 737288 | tf_op jit(solution)/shard_map/ppermute | solution.py:26
  78.7 10.3 %collective-permute-start.17 = (f32[1,120,512]{2,1,0:T(8,128)S(1)}, f32[1,120,512]{2,1,0:T(8,128)S(1)}, u32[]{:S(2)}, u32[]{:S(2)}) collective-permute-start(f32[1,120,512]{2,1,0:T(8,128)S(1)} %get-tuple-element.122.refs_0_), channel_id=1, source_target_pairs={{0,16},{4,20},{8,24},{12,28},{16,0},{20,4},{24,8},{28,12},{1,17},{... | collective-permute-start | bytes 737288 | tf_op jit(solution)/shard_map/ppermute | solution.py:26
